TPU v7x, 512 devices: a whole 4x8x8 slice. The times are simulated.
512 devices in a mesh: rad: 32 (over z_hi, x, core), lat: 16 (over z_lo, y).
Axes of the slice: x: 4, y: 8, z: 8 (z_hi: 4, z_lo: 2; z = z_hi * 2 + z_lo), core: 2. Of those that a mesh axis runs over, the one named last changes fastest.
Arguments:
- nonlinear_samples: bfloat16 [32, 2, 1536, 3072], P('rad', None, 'lat'), may hold values from -6 to 6
- legendre: bfloat16 [256, 1536, 1024], P('rad', 'lat'), may hold values from -0.21875 to 0.21875
- assign: int32 [256], replicated, may hold values from 0 to 255, each once
- counts: int32 [256], replicated, may hold values from 513 to 1024, as said below
- spectral_state: float32 [1024, 256, 128], P('lat', 'rad'), may hold values from -6 to 6
- inverses: float32 [1024, 4, 8, 8], P('lat'), may hold values from -1 to 1
Outputs:
- advanced: float32 [1024, 256, 128], P('lat', 'rad')
Inputs may be any that keep to these rules, and one draw needn't show every extreme that they name: Slot s carries order assign[s]; each order 0 to 255 stands in exactly one slot. counts[m] is at most 1024 - m, and order 0 has 1024 live degrees.
All inputs are finite; a program needn't handle non-finite values.
Results may differ from a plain program's by a relative error of at most 0.0034.
Values may be sent and summed in bfloat16 or wider, within the bound.
A program may use at most 64 MiB of HBM per device.

v0:
```python
import math
import jax
import jax.numpy as jnp
from jax import lax
from jax.sharding import PartitionSpec as P


def trig_table(assign, lon_count):
    longitude = jnp.arange(lon_count, dtype=jnp.int32)
    phases = longitude[:, None] * assign[None, :] % lon_count
    angles = phases.astype(jnp.float32) * (2.0 * math.pi / lon_count)
    normalizing_multiplier = 1.0 / math.sqrt(lon_count)
    cosine = (jnp.cos(angles) * normalizing_multiplier).astype(jnp.bfloat16)
    sine = (-jnp.sin(angles) * normalizing_multiplier).astype(jnp.bfloat16)
    return jnp.stack([cosine, sine], axis=2).reshape(lon_count, 2 * assign.shape[0])


def radial_step(spectral_state, source, inverses, degree):
    deg_rows, slot_count, width = spectral_state.shape
    shell_number = width // 4
    blk_size = inverses.shape[2]
    blk_count = shell_number // blk_size
    field_now = spectral_state.reshape(deg_rows, slot_count, 4, shell_number)
    zero_rim = jnp.zeros((deg_rows, slot_count, 4, 1), jnp.float32)
    outward = jnp.concatenate([field_now[..., 1:], zero_rim], axis=3)
    inward = jnp.concatenate([zero_rim, field_now[..., :-1]], axis=3)
    radial_spacing = 0.65 / (shell_number + 1)
    radius = 0.35 + 0.65 * (jnp.arange(shell_number, dtype=jnp.float32) + 1.0) / (shell_number + 1)
    ratios = radial_spacing / radius
    degree_term = degree[:, None, None, None] * (degree[:, None, None, None] + 1.0)
    central = 0.5 * radial_spacing * radial_spacing * degree_term / (radius * radius)
    right_side = (
        field_now + 0.5 * (outward - 2.0 * field_now + inward) + 0.5 * ratios * (outward - inward)
    )
    right_side = (
        right_side - central * field_now + source.reshape(deg_rows, slot_count, 4, shell_number)
    )
    lower_link = -0.5 * (1.0 - ratios[0::blk_size])
    upper_link = -0.5 * (1.0 + ratios[blk_size - 1 :: blk_size])
    blocks = jnp.moveaxis(right_side.reshape(deg_rows, slot_count, 4, blk_count, blk_size), 3, 0)
    block_inverse = jnp.moveaxis(inverses, 1, 0)
    first_unit = (jnp.arange(blk_size, dtype=jnp.int32) == 0).astype(jnp.float32)
    start_carry = jnp.zeros((deg_rows, slot_count, 4), jnp.float32)

    def forward(carried, items):
        matrix, block, link = items
        block = block - link * carried[..., None] * first_unit
        result = jnp.einsum("lij,locj->loci", matrix, block, precision=lax.Precision.HIGHEST)
        return (result[..., blk_size - 1], result)

    def inverse_sweep(carried, items):
        matrix, partial_solution, link = items
        result = (
            partial_solution - link * carried[..., None] * matrix[:, None, None, :, blk_size - 1]
        )
        return (result[..., 0], result)

    _, forward_blocks = lax.scan(forward, start_carry, (block_inverse, blocks, lower_link))
    _, solved = lax.scan(
        inverse_sweep, start_carry, (block_inverse, forward_blocks, upper_link), reverse=True
    )
    return jnp.moveaxis(solved, 0, 3).reshape(deg_rows, slot_count, 4 * shell_number)


def body(nonlinear_samples, legendre, assign, counts, spectral_state, inverses):
    rad_local = nonlinear_samples.shape[0]
    lat_local = nonlinear_samples.shape[2]
    lon_count = nonlinear_samples.shape[3]
    order_total = assign.shape[0]
    order_local = legendre.shape[0]
    degree_local = spectral_state.shape[0]
    shell_grand_number = spectral_state.shape[2] // 4
    table = trig_table(assign, lon_count)
    flat_rows = nonlinear_samples.reshape(rad_local * 2 * lat_local, lon_count)
    fourier_modes = jnp.dot(flat_rows, table, preferred_element_type=jnp.float32).astype(
        jnp.bfloat16
    )
    fourier_modes = fourier_modes.reshape(rad_local, 2, lat_local, order_total, 2)
    thermal_part = lax.all_to_all(
        fourier_modes[:, 0], "rad", split_axis=2, concat_axis=0, tiled=True
    )
    magnetic_potential_part = lax.all_to_all(
        fourier_modes[:, 1], "rad", split_axis=2, concat_axis=0, tiled=True
    )
    permuted_dims = jnp.stack([thermal_part, magnetic_potential_part], axis=1)
    columns = lax.all_to_all(legendre, "lat", split_axis=2, concat_axis=1, tiled=True)
    whole = lax.all_gather(permuted_dims, "lat", axis=2, tiled=True)
    band_total = lax.axis_size("lat")
    legendre_table_bands = columns.reshape(order_local, band_total, lat_local, degree_local)
    value_bands = whole.reshape(shell_grand_number, 2, band_total, lat_local, order_local, 2)
    partial_value = jnp.einsum(
        "obtl,rfbtok->blofkr", legendre_table_bands, value_bands, preferred_element_type=jnp.float32
    )
    partial_value = lax.optimization_barrier(partial_value.astype(jnp.bfloat16)).astype(jnp.float32)
    summed = jnp.sum(partial_value, axis=0).reshape(
        degree_local, order_local, 4 * shell_grand_number
    )
    rad_position = lax.axis_index("rad")
    lat_position = lax.axis_index("lat")
    my_orders = lax.dynamic_slice_in_dim(assign, rad_position * order_local, order_local, 0)
    order_ids = jnp.arange(order_total, dtype=jnp.int32)
    my_counts = jnp.sum(
        jnp.where(my_orders[:, None] == order_ids[None, :], counts[None, :], 0), axis=1
    )
    degree_ids = lat_position * degree_local + jnp.arange(degree_local, dtype=jnp.int32)
    limits = my_orders + my_counts
    live = (degree_ids[:, None] >= my_orders[None, :]) & (degree_ids[:, None] < limits[None, :])
    source = jnp.where(live[:, :, None], summed, jnp.zeros_like(summed))
    return radial_step(spectral_state, source, inverses, degree_ids.astype(jnp.float32))


def solution(mesh):
    return jax.shard_map(
        body,
        mesh=mesh,
        in_specs=(
            P("rad", None, "lat", None),
            P("rad", "lat", None),
            P(),
            P(),
            P("lat", "rad", None),
            P("lat", None, None, None),
        ),
        out_specs=P("lat", "rad", None),
        check_vma=False,
    )
```

profile of v0, /device:TPU:1, one launch (start us, length us, event | category | flops | bytes accessed | tf_op | source)
XLA Modules:
  0.0 378.4 jit_solution(9484199052676013640)
XLA Ops:
  6.5 14.2 %multiply_convert_fusion.1 = (bf16[3072,256,1]{1,0,2:T(8,128)(2,1)S(1)}, bf16[3072,256,1]{1,0,2:T(8,128)(2,1)S(1)}) fusion(s32[256]{0:T(256)} %param.12), kind=kLoop, calls=%fused_computation.29 | loop fusion | flops 11010048 | bytes 3146752 | tf_op jit(solution)/shard_map/convert_element_type | solution.py:13
  20.7 1.9 pad_maximum_fusion
  22.7 8.8 %copy.108 = bf16[3072,256,2]{0,2,1:T(2,128)(2,1)} copy(bf16[3072,256,2]{1,0,2:T(8,128)(2,1)} %pad_maximum_fusion) | data formatting | bytes 6291456 | tf_op jit(solution)/shard_map/stack | solution.py:15
  31.4 7.5 %reshape.244 = bf16[3072,512]{0,1:T(8,128)(2,1)} reshape(bf16[3072,256,2]{0,2,1:T(2,128)(2,1)} %copy.108) | data formatting | bytes 6291456 | tf_op jit(solution)/shard_map/reshape | solution.py:15
  38.9 3.1 fusion.20
  42.9 0.8 copy.114
  43.6 14.4 %all-to-all-start.1 = ((bf16[1,96,256,2]{1,3,0,2:T(2,128)(2,1)}), bf16[1,96,256,2]{1,3,0,2:T(2,128)(2,1)S(1)}, u32[]{:S(2)}, u32[]{:S(2)}) async-start(bf16[1,96,256,2]{1,3,0,2:T(2,128)(2,1)} %copy.114), calls=%async_computation.1 | async-start | bytes 262144 | tf_op jit(solution)/shard_map/all_to_all | solution.py:82
  58.2 0.8 copy.111
  59.0 10.4 %all-to-all-done.1 = bf16[1,96,256,2]{1,3,0,2:T(2,128)(2,1)S(1)} async-done(((bf16[1,96,256,2]{1,3,0,2:T(2,128)(2,1)}), bf16[1,96,256,2]{1,3,0,2:T(2,128)(2,1)S(1)}, u32[]{:S(2)}, u32[]{:S(2)}) %all-to-all-start.1) | async-done | bytes 98336 | tf_op jit(solution)/shard_map/all_to_all | solution.py:82
  69.4 3.7 all-to-all-start
  73.2 11.1 %all-to-all-done = bf16[1,96,256,2]{1,3,0,2:T(2,128)(2,1)S(1)} async-done(((bf16[1,96,256,2]{1,3,0,2:T(2,128)(2,1)}), bf16[1,96,256,2]{1,3,0,2:T(2,128)(2,1)S(1)}, u32[]{:S(2)}, u32[]{:S(2)}) %all-to-all-start) | async-done | bytes 98336 | tf_op jit(solution)/shard_map/all_to_all | solution.py:79
  84.3 2.2 copy.116
  86.6 2.9 copy.118
  89.5 7.4 %all-to-all-start.2 = ((bf16[8,96,1024]{1,0,2:T(8,128)(2,1)}), bf16[8,96,1024]{1,0,2:T(8,128)(2,1)}, u32[]{:S(2)}, u32[]{:S(2)}) async-start(bf16[8,96,1024]{1,0,2:T(8,128)(2,1)} %copy.118), calls=%async_computation.2 | async-start | bytes 4194304 | tf_op jit(solution)/shard_map/all_to_all | solution.py:86
  97.4 1.3 copy.122
  99.3 70.4 %all-to-all-done.2 = bf16[8,96,1024]{1,0,2:T(8,128)(2,1)} async-done(((bf16[8,96,1024]{1,0,2:T(8,128)(2,1)}), bf16[8,96,1024]{1,0,2:T(8,128)(2,1)}, u32[]{:S(2)}, u32[]{:S(2)}) %all-to-all-start.2) | async-done | bytes 1572896 | tf_op jit(solution)/shard_map/all_to_all | solution.py:86
  169.7 102.0 %all-gather.2.cloned.1.call-done = bf16[32,2,1536,8,2]{0,3,4,1,2:T(8,128)(2,1)} async-done(((bf16[32,2,96,8,2]{0,3,4,1,2:T(8,128)(2,1)}), bf16[32,2,1536,8,2]{0,3,4,1,2:T(8,128)(2,1)}) %all-gather.2.cloned.1.call-update) | async-done | bytes 3145744 | tf_op jit(solution)/shard_map/all_gather | solution.py:87
  271.8 8.7 %convert_bitcast_fusion = bf16[16,64,8,2,2,32]{1,5,4,3,2,0:T(8,128)(2,1)S(1)} fusion(bf16[32,2,16,96,8,2]{0,4,5,1,3,2:T(8,128)(2,1)} %bitcast.114, bf16[8,96,16,64]{1,0,3,2:T(8,128)(2,1)} %bitcast.15), kind=kOutput, calls=%fused_computation.24 | convolution fusion | flops 202375168 | bytes 6815744 | tf_op jit(solution)/shard_map/obtl,rfbtok->blofkr/dot_general | solution.py:91
  280.5 1.0 convert_reduce_fusion
  281.4 1.1 add_bitcast_fusion
  282.5 0.9 broadcast.271.clone2
  283.4 77.8 %while.30 = (s32[]{:T(128)}, f32[64,8,4]{1,2,0:T(4,128)S(1)}, f32[4,64,8,4,8]{1,4,3,2,0:T(8,128)}, f32[4,64,8,4,8]{1,4,0,3,2:T(8,128)}, f32[4]{0:T(128)S(1)}, /*index=5*/f32[4,64,8,8]{3,2,1,0:T(8,128)}, s32[]{:T(128)}) while((s32[]{:T(128)}, f32[64,8,4]{1,2,0:T(4,128)S(1)}, f32[4,64,8,4,8]{1,4,3,2,0:T(8,128)}, ...), condition=%wide.region_3.4_spmd.clone, body=%wide.region_2.3_spmd.clone.sunk | while | flops 1607698 | bytes 1025185 | solution.py:58
  283.4 0.9 constant_dynamic-slice_fusion.5
  284.4 0.9 copy.162
  286.5 14.9 %fusion.30 = f32[64,8,4,8]{1,3,2,0:T(8,128)S(1)} fusion(f32[1,64,8,4,8]{4,2,3,1,0:T(8,128)S(1)} %copy.162, f32[8]{0:T(128)S(1)} %compare_convert_fusion.2, f32[64,8,4]{1,2,0:T(4,128)S(1)} %bitcast.101, f32[4,64,8,8]{3,2,1,0:T(8,128)} %get-tuple-element.387, s32[]{:T(128)} %get-tuple-element.375), kind=kOutput, calls=%fused_computation.9.clone.1 | convolution fusion | flops 1605632 | bytes 401952 | tf_op jit(solution)/shard_map/while/body/eval_jaxpr/lij,locj->loci/dot_general | solution.py:48
  302.1 0.7 constant_dynamic-update-slice_fusion.2
  302.9 0.9 constant_dynamic-slice_fusion.5
  303.8 0.9 copy.162
  306.0 14.9 %fusion.30 = f32[64,8,4,8]{1,3,2,0:T(8,128)S(1)} fusion(f32[1,64,8,4,8]{4,2,3,1,0:T(8,128)S(1)} %copy.162, f32[8]{0:T(128)S(1)} %compare_convert_fusion.2, f32[64,8,4]{1,2,0:T(4,128)S(1)} %bitcast.101, f32[4,64,8,8]{3,2,1,0:T(8,128)} %get-tuple-element.387, s32[]{:T(128)} %get-tuple-element.375), kind=kOutput, calls=%fused_computation.9.clone.1 | convolution fusion | flops 1605632 | bytes 401952 | tf_op jit(solution)/shard_map/while/body/eval_jaxpr/lij,locj->loci/dot_general | solution.py:48
  321.5 0.7 constant_dynamic-update-slice_fusion.2
  322.3 0.9 constant_dynamic-slice_fusion.5
  323.3 0.9 copy.162
  325.4 14.9 %fusion.30 = f32[64,8,4,8]{1,3,2,0:T(8,128)S(1)} fusion(f32[1,64,8,4,8]{4,2,3,1,0:T(8,128)S(1)} %copy.162, f32[8]{0:T(128)S(1)} %compare_convert_fusion.2, f32[64,8,4]{1,2,0:T(4,128)S(1)} %bitcast.101, f32[4,64,8,8]{3,2,1,0:T(8,128)} %get-tuple-element.387, s32[]{:T(128)} %get-tuple-element.375), kind=kOutput, calls=%fused_computation.9.clone.1 | convolution fusion | flops 1605632 | bytes 401952 | tf_op jit(solution)/shard_map/while/body/eval_jaxpr/lij,locj->loci/dot_general | solution.py:48
  341.0 0.7 constant_dynamic-update-slice_fusion.2
  341.8 0.9 constant_dynamic-slice_fusion.5
  342.7 0.9 copy.162
  344.9 14.9 %fusion.30 = f32[64,8,4,8]{1,3,2,0:T(8,128)S(1)} fusion(f32[1,64,8,4,8]{4,2,3,1,0:T(8,128)S(1)} %copy.162, f32[8]{0:T(128)S(1)} %compare_convert_fusion.2, f32[64,8,4]{1,2,0:T(4,128)S(1)} %bitcast.101, f32[4,64,8,8]{3,2,1,0:T(8,128)} %get-tuple-element.387, s32[]{:T(128)} %get-tuple-element.375), kind=kOutput, calls=%fused_computation.9.clone.1 | convolution fusion | flops 1605632 | bytes 401952 | tf_op jit(solution)/shard_map/while/body/eval_jaxpr/lij,locj->loci/dot_general | solution.py:48
  360.4 0.7 constant_dynamic-update-slice_fusion.2
  361.3 9.2 %while.29 = (s32[]{:T(128)}, f32[64,8,4]{0,2,1:T(4,128)S(1)}, f32[4,64,8,4,8]{1,4,3,2,0:T(8,128)S(1)}, f32[4,64,8,4,8]{1,4,3,2,0:T(8,128)}, f32[4]{0:T(128)S(1)}...) while((s32[]{:T(128)}, f32[64,8,4]{0,2,1:T(4,128)S(1)}, f32[4,64,8,4,8]{1,4,3,2,0:T(8,128)S(1)}, ...), condition=%wide.region_5.6_spmd, body=%wide.region_4.5_spmd.sunk | while | flops 38915 | bytes 459641 | solution.py:59
  361.4 0.7 dynamic_slice.63
  362.6 0.9 subtract_dynamic-update-slice_fusion.2
  363.7 0.7 dynamic_slice.63
  364.9 0.9 subtract_dynamic-update-slice_fusion.2
  366.0 0.7 dynamic_slice.63
  367.3 0.9 subtract_dynamic-update-slice_fusion.2
  368.3 0.7 dynamic_slice.63
  369.6 0.9 subtract_dynamic-update-slice_fusion.2
  370.6 0.9 copy.129
  (86 shorter events, 12.9 us)
Async XLA Ops:
  6.5 32.4 %copy-start = (bf16[1,2,96,3072]{3,2,1,0:T(8,128)(2,1)S(1)}, bf16[1,2,96,3072]{3,2,1,0:T(8,128)(2,1)}, u32[]{:S(2)}) copy-start(bf16[1,2,96,3072]{3,2,1,0:T(8,128)(2,1)} %param.10) | copy-start | bytes 3538948
  42.2 44.4 %copy-start.1 = (bf16[8,96,1024]{2,1,0:T(8,128)(2,1)S(1)}, bf16[8,96,1024]{2,1,0:T(8,128)(2,1)}, u32[]{:S(2)}) copy-start(bf16[8,96,1024]{2,1,0:T(8,128)(2,1)} %param.11) | copy-start | bytes 4718596
  43.6 25.8 %all-to-all-start.1 = ((bf16[1,96,256,2]{1,3,0,2:T(2,128)(2,1)}), bf16[1,96,256,2]{1,3,0,2:T(2,128)(2,1)S(1)}, u32[]{:S(2)}, u32[]{:S(2)}) async-start(bf16[1,96,256,2]{1,3,0,2:T(2,128)(2,1)} %copy.114), calls=%async_computation.1 | async-start | bytes 262144 | tf_op jit(solution)/shard_map/all_to_all | solution.py:82
  69.4 14.8 %all-to-all-start = ((bf16[1,96,256,2]{1,3,0,2:T(2,128)(2,1)}), bf16[1,96,256,2]{1,3,0,2:T(2,128)(2,1)S(1)}, u32[]{:S(2)}, u32[]{:S(2)}) async-start(bf16[1,96,256,2]{1,3,0,2:T(2,128)(2,1)} %copy.111), calls=%async_computation | async-start | bytes 262144 | tf_op jit(solution)/shard_map/all_to_all | solution.py:79
  73.1 198.7 %all-gather.2.cloned.1.call-start = ((), (), s32[]{:S(2)}) async-start(), calls=%async_computation.3 | async-start | bytes 13369344 | tf_op jit(solution)/shard_map/all_gather | solution.py:87
  86.5 10.5 %copy-start.4 = (s32[256]{0:T(256)S(1)}, s32[256]{0:T(256)}, u32[]{:S(2)}) copy-start(s32[256]{0:T(256)} %param.12) | copy-start | bytes 3076
  86.6 10.6 %copy-start.3 = (f32[64,8,128]{2,1,0:T(8,128)S(1)}, f32[64,8,128]{2,1,0:T(8,128)}, u32[]{:S(2)}) copy-start(f32[64,8,128]{2,1,0:T(8,128)} %param.14) | copy-start | bytes 786436
  89.4 7.9 %copy-start.2 = (f32[64,4,8,8]{0,3,2,1:T(8,128)S(1)}, f32[64,4,8,8]{0,3,2,1:T(8,128)}, u32[]{:S(2)}) copy-start(f32[64,4,8,8]{0,3,2,1:T(8,128)} %param.15) | copy-start | bytes 196612
  89.5 9.3 %copy-start.5 = (s32[256]{0:T(256)S(1)}, s32[256]{0:T(256)}, u32[]{:S(2)}) copy-start(s32[256]{0:T(256)} %param.13) | copy-start | bytes 3076
  89.5 80.3 %all-to-all-start.2 = ((bf16[8,96,1024]{1,0,2:T(8,128)(2,1)}), bf16[8,96,1024]{1,0,2:T(8,128)(2,1)}, u32[]{:S(2)}, u32[]{:S(2)}) async-start(bf16[8,96,1024]{1,0,2:T(8,128)(2,1)} %copy.118), calls=%async_computation.2 | async-start | bytes 4194304 | tf_op jit(solution)/shard_map/all_to_all | solution.py:86
Sparse Core Ops, SparseCore 0:
  86.7 185.0 all-gather.1
where the time goes:
time: 379 us; the launch traced here: 378 us
  waiting for transfers between devices  194 us (51%)
  matrix products  71.3 us (19%)
  local copies, waits for them, and re-layouts  45.8 us (12%)
  other arithmetic  27.6 us (7%)
  starting transfers between devices  25.5 us (7%)
  between operations  13.6 us (4%)
    all_gather x1, waiting for transfers between devices, body(): whole = lax.all_gather(permuted_dims, 'lat', axis=2, tiled=True)  102 us
    all_to_all x1, waiting for transfers between devices, body(): lax.all_to_all(legendre, 'lat', split_axis=2, concat_axis=1, tiled=True)  70.4 us
    dot_general x4, matrix products, forward(): jnp.einsum('lij,locj->loci', matrix, block, precision=lax.Precision.HIGHEST)  59.6 us
    all_to_all x1, starting transfers between devices, body(): lax.all_to_all(fourier_modes[:, 1], 'rad', split_axis=2, concat_axis=0, t...  14.4 us
    convert_element_type x1, other arithmetic, trig_table(): cosine = (jnp.cos(angles) * normalizing_multiplier).astype(jnp.bfloat16)  14.2 us
    dynamic_slice x24, local copies, waits for them, and re-layouts, radial_step(): lax.scan(forward, start_carry, (block_inverse, blocks, lower_link))  12.4 us
    all_to_all x1, waiting for transfers between devices, body(): lax.all_to_all(fourier_modes[:, 0], 'rad', split_axis=2, concat_axis=0, t...  11.1 us
    all_to_all x1, waiting for transfers between devices, body(): lax.all_to_all(fourier_modes[:, 1], 'rad', split_axis=2, concat_axis=0, t...  10.4 us
  transfers between devices with their start and end apart: 4, of which 4 were waited for; matrix products, arithmetic and copies ran while one was open for 2% of the time, Pallas kernels for 0%

commit v1 on v0

--- a/solution.py
+++ b/solution.py
@@ -84,7 +84,9 @@
     )
     permuted_dims = jnp.stack([thermal_part, magnetic_potential_part], axis=1)
     columns = lax.all_to_all(legendre, "lat", split_axis=2, concat_axis=1, tiled=True)
-    whole = lax.all_gather(permuted_dims, "lat", axis=2, tiled=True)
+    whole = jnp.concatenate(
+        lax.all_to_all(jnp.stack([permuted_dims] * lax.axis_size("lat")), "lat", 0, 0), axis=2
+    )
     band_total = lax.axis_size("lat")
     legendre_table_bands = columns.reshape(order_local, band_total, lat_local, degree_local)
     value_bands = whole.reshape(shell_grand_number, 2, band_total, lat_local, order_local, 2)

time: 379 us -> 336 us (0.89)
  waiting for transfers between devices: 194 us -> 155 us
  between operations: 13.6 us -> 0.25 us
  starting transfers between devices: 25.5 us -> 32 us
  local copies, waits for them, and re-layouts: 45.8 us -> 51.2 us
  matrix products: 71.3 us -> 66.2 us
    all_gather x1 -> x0, waiting for transfers between devices: 102 us -> none  [body(): whole = lax.all_gather(permuted_dims, 'lat', axis=2, tiled=True)]
    all_to_all x0 -> x1, waiting for transfers between devices: none -> 88.2 us  [body(): lax.all_to_all(jnp.stack([permuted_dims] * lax.axis_size('lat')), 'lat',...]
    all_to_all x1, waiting for transfers between devices: 70.4 us -> 48.4 us  [body(): lax.all_to_all(legendre, 'lat', split_axis=2, concat_axis=1, tiled=True)]
    all_to_all x0 -> x1, starting transfers between devices: none -> 6.67 us  [body(): lax.all_to_all(jnp.stack([permuted_dims] * lax.axis_size('lat')), 'lat',...]
    dot_general x1, matrix products: 8.66 us -> 3.43 us  [body(): jnp.einsum('obtl,rfbtok->blofkr', legendre_table_bands, value_bands, pref...]
  transfers between devices with their start and end apart: 4 -> 4, of which waited for: 4 -> 4; matrix products, arithmetic and copies ran while one was open for 2% -> 3% of each run, Pallas kernels for 0% -> 0%
where the time goes in v1:
time: 336 us; the launch traced here: 333 us
  waiting for transfers between devices  155 us (46%)
  matrix products  66.2 us (20%)
  local copies, waits for them, and re-layouts  51.2 us (15%)
  starting transfers between devices  32 us (10%)
  other arithmetic  27.6 us (8%)
    all_to_all x1, waiting for transfers between devices, body(): lax.all_to_all(jnp.stack([permuted_dims] * lax.axis_size('lat')), 'lat',...  88.2 us
    dot_general x4, matrix products, forward(): jnp.einsum('lij,locj->loci', matrix, block, precision=lax.Precision.HIGHEST)  59.6 us
    all_to_all x1, waiting for transfers between devices, body(): lax.all_to_all(legendre, 'lat', split_axis=2, concat_axis=1, tiled=True)  48.4 us
    all_to_all x1, starting transfers between devices, body(): lax.all_to_all(fourier_modes[:, 1], 'rad', split_axis=2, concat_axis=0, t...  14.4 us
    convert_element_type x1, other arithmetic, trig_table(): cosine = (jnp.cos(angles) * normalizing_multiplier).astype(jnp.bfloat16)  14.2 us
    dynamic_slice x24, local copies, waits for them, and re-layouts, radial_step(): lax.scan(forward, start_carry, (block_inverse, blocks, lower_link))  12.4 us
    all_to_all x1, waiting for transfers between devices, body(): lax.all_to_all(fourier_modes[:, 1], 'rad', split_axis=2, concat_axis=0, t...  10.4 us
    another operation x1, local copies, waits for them, and re-layouts, trig_table(): jnp.stack([cosine, sine], axis=2).reshape(lon_count, 2 * assign.shape[0])  8.78 us
  transfers between devices with their start and end apart: 4, of which 4 were waited for; matrix products, arithmetic and copies ran while one was open for 3% of the time, Pallas kernels for 0%

profile of v1, /device:TPU:1, one launch (start us, length us, event | category | flops | bytes accessed | tf_op | source)
XLA Modules:
  0.0 333.2 jit_solution(13857959219880809567)
XLA Ops:
  0.0 14.2 %multiply_convert_fusion.1 = (bf16[3072,256,1]{1,0,2:T(8,128)(2,1)S(1)}, bf16[3072,256,1]{1,0,2:T(8,128)(2,1)S(1)}) fusion(s32[256]{0:T(256)} %param.12), kind=kLoop, calls=%fused_computation.29 | loop fusion | flops 11010048 | bytes 3146752 | tf_op jit(solution)/shard_map/convert_element_type | solution.py:13
  14.2 2.0 pad_maximum_fusion
  16.1 8.8 %copy.103 = bf16[3072,256,2]{0,2,1:T(2,128)(2,1)} copy(bf16[3072,256,2]{1,0,2:T(8,128)(2,1)} %pad_maximum_fusion) | data formatting | bytes 6291456 | tf_op jit(solution)/shard_map/stack | solution.py:15
  24.9 7.5 %reshape.246 = bf16[3072,512]{0,1:T(8,128)(2,1)} reshape(bf16[3072,256,2]{0,2,1:T(2,128)(2,1)} %copy.103) | data formatting | bytes 6291456 | tf_op jit(solution)/shard_map/reshape | solution.py:15
  32.4 3.2 fusion.20
  36.5 0.8 copy.109
  37.2 14.4 %all-to-all-start.1 = ((bf16[1,96,256,2]{1,3,0,2:T(2,128)(2,1)}), bf16[1,96,256,2]{1,3,0,2:T(2,128)(2,1)S(1)}, u32[]{:S(2)}, u32[]{:S(2)}) async-start(bf16[1,96,256,2]{1,3,0,2:T(2,128)(2,1)} %copy.109), calls=%async_computation.1 | async-start | bytes 262144 | tf_op jit(solution)/shard_map/all_to_all | solution.py:82
  51.8 0.8 copy.106
  52.6 10.4 %all-to-all-done.1 = bf16[1,96,256,2]{1,3,0,2:T(2,128)(2,1)S(1)} async-done(((bf16[1,96,256,2]{1,3,0,2:T(2,128)(2,1)}), bf16[1,96,256,2]{1,3,0,2:T(2,128)(2,1)S(1)}, u32[]{:S(2)}, u32[]{:S(2)}) %all-to-all-start.1) | async-done | bytes 98336 | tf_op jit(solution)/shard_map/all_to_all | solution.py:82
  63.0 3.7 %all-to-all-start = ((bf16[1,96,256,2]{1,3,0,2:T(2,128)(2,1)}), bf16[1,96,256,2]{1,3,0,2:T(2,128)(2,1)S(1)}, u32[]{:S(2)}, u32[]{:S(2)}) async-start(bf16[1,96,256,2]{1,3,0,2:T(2,128)(2,1)} %copy.106), calls=%async_computation | async-start | bytes 262144 | tf_op jit(solution)/shard_map/all_to_all | solution.py:79
  66.7 2.9 copy.112
  69.6 8.2 %all-to-all-done = bf16[1,96,256,2]{1,3,0,2:T(2,128)(2,1)S(1)} async-done(((bf16[1,96,256,2]{1,3,0,2:T(2,128)(2,1)}), bf16[1,96,256,2]{1,3,0,2:T(2,128)(2,1)S(1)}, u32[]{:S(2)}, u32[]{:S(2)}) %all-to-all-start) | async-done | bytes 98336 | tf_op jit(solution)/shard_map/all_to_all | solution.py:79
  77.8 7.2 %all-to-all-start.3 = ((bf16[8,96,1024]{1,0,2:T(8,128)(2,1)}), bf16[8,96,1024]{1,0,2:T(8,128)(2,1)S(1)}, u32[]{:S(2)}, u32[]{:S(2)}) async-start(bf16[8,96,1024]{1,0,2:T(8,128)(2,1)} %copy.112), calls=%async_computation.3 | async-start | bytes 4194304 | tf_op jit(solution)/shard_map/all_to_all | solution.py:86
  85.2 48.4 %all-to-all-done.3 = bf16[8,96,1024]{1,0,2:T(8,128)(2,1)S(1)} async-done(((bf16[8,96,1024]{1,0,2:T(8,128)(2,1)}), bf16[8,96,1024]{1,0,2:T(8,128)(2,1)S(1)}, u32[]{:S(2)}, u32[]{:S(2)}) %all-to-all-start.3) | async-done | bytes 1572896 | tf_op jit(solution)/shard_map/all_to_all | solution.py:86
  133.6 3.0 stack.8
  136.6 6.7 %all-to-all-start.2 = ((bf16[16,32,2,96,8,2]{3,1,5,2,4,0:T(8,128)(2,1)}), bf16[16,32,2,96,8,2]{3,1,5,2,4,0:T(8,128)(2,1)}, u32[]{:S(2)}, u32[]{:S(2)}) async-start(bf16[16,32,2,96,8,2]{3,1,5,2,4,0:T(8,128)(2,1)} %stack.8), calls=%async_computation.2 | async-start | bytes 8388608 | tf_op jit(solution)/shard_map/all_to_all | solution.py:88
  143.6 2.0 copy.102
  145.6 1.4 copy.115
  147.5 2.3 fusion.23
  149.8 88.2 %all-to-all-done.2 = bf16[16,32,2,96,8,2]{3,1,5,2,4,0:T(8,128)(2,1)} async-done(((bf16[16,32,2,96,8,2]{3,1,5,2,4,0:T(8,128)(2,1)}), bf16[16,32,2,96,8,2]{3,1,5,2,4,0:T(8,128)(2,1)}, u32[]{:S(2)}, u32[]{:S(2)}) %all-to-all-start.2) | async-done | bytes 3145760 | tf_op jit(solution)/shard_map/all_to_all | solution.py:88
  238.1 3.4 %convert_bitcast_fusion = bf16[16,64,8,2,2,32]{1,5,4,3,2,0:T(8,128)(2,1)S(1)} fusion(bf16[16,32,2,96,8,2]{3,1,5,2,4,0:T(8,128)(2,1)} %all-to-all-done.2, bf16[8,96,16,64]{1,0,3,2:T(8,128)(2,1)S(1)} %bitcast.99), kind=kOutput, calls=%fused_computation.24 | convolution fusion | flops 202375168 | bytes 6815744 | tf_op jit(solution)/shard_map/obtl,rfbtok->blofkr/dot_general | solution.py:93
  241.5 1.0 convert_reduce_fusion
  242.9 1.1 add_bitcast_fusion
  244.0 0.9 broadcast.273.clone2
  244.8 78.2 %while.30 = (s32[]{:T(128)}, f32[64,8,4]{1,2,0:T(4,128)S(1)}, f32[4,64,8,4,8]{1,4,3,2,0:T(8,128)}, f32[4,64,8,4,8]{1,4,0,3,2:T(8,128)}, f32[4]{0:T(128)S(1)}, /*index=5*/f32[4,64,8,8]{3,2,1,0:T(8,128)}, s32[]{:T(128)}) while((s32[]{:T(128)}, f32[64,8,4]{1,2,0:T(4,128)S(1)}, f32[4,64,8,4,8]{1,4,3,2,0:T(8,128)}, ...), condition=%wide.region_3.4_spmd.clone, body=%wide.region_2.3_spmd.clone.sunk | while | flops 1607698 | bytes 1025185 | solution.py:58
  245.0 0.9 constant_dynamic-slice_fusion.5
  246.0 0.9 copy.149
  248.2 14.9 %fusion.30 = f32[64,8,4,8]{1,3,2,0:T(8,128)S(1)} fusion(f32[1,64,8,4,8]{4,2,3,1,0:T(8,128)S(1)} %copy.149, f32[8]{0:T(128)S(1)} %compare_convert_fusion.2, f32[64,8,4]{1,2,0:T(4,128)S(1)} %bitcast.106, f32[4,64,8,8]{3,2,1,0:T(8,128)} %get-tuple-element.387, s32[]{:T(128)} %get-tuple-element.375), kind=kOutput, calls=%fused_computation.9.clone.1 | convolution fusion | flops 1605632 | bytes 401952 | tf_op jit(solution)/shard_map/while/body/eval_jaxpr/lij,locj->loci/dot_general | solution.py:48
  263.7 0.7 constant_dynamic-update-slice_fusion.2
  264.5 0.9 constant_dynamic-slice_fusion.5
  265.5 0.9 copy.149
  267.7 14.9 %fusion.30 = f32[64,8,4,8]{1,3,2,0:T(8,128)S(1)} fusion(f32[1,64,8,4,8]{4,2,3,1,0:T(8,128)S(1)} %copy.149, f32[8]{0:T(128)S(1)} %compare_convert_fusion.2, f32[64,8,4]{1,2,0:T(4,128)S(1)} %bitcast.106, f32[4,64,8,8]{3,2,1,0:T(8,128)} %get-tuple-element.387, s32[]{:T(128)} %get-tuple-element.375), kind=kOutput, calls=%fused_computation.9.clone.1 | convolution fusion | flops 1605632 | bytes 401952 | tf_op jit(solution)/shard_map/while/body/eval_jaxpr/lij,locj->loci/dot_general | solution.py:48
  283.2 0.7 constant_dynamic-update-slice_fusion.2
  284.0 0.9 constant_dynamic-slice_fusion.5
  285.0 0.9 copy.149
  285.9 0.6 dynamic_slice.66
  287.2 14.9 %fusion.30 = f32[64,8,4,8]{1,3,2,0:T(8,128)S(1)} fusion(f32[1,64,8,4,8]{4,2,3,1,0:T(8,128)S(1)} %copy.149, f32[8]{0:T(128)S(1)} %compare_convert_fusion.2, f32[64,8,4]{1,2,0:T(4,128)S(1)} %bitcast.106, f32[4,64,8,8]{3,2,1,0:T(8,128)} %get-tuple-element.387, s32[]{:T(128)} %get-tuple-element.375), kind=kOutput, calls=%fused_computation.9.clone.1 | convolution fusion | flops 1605632 | bytes 401952 | tf_op jit(solution)/shard_map/while/body/eval_jaxpr/lij,locj->loci/dot_general | solution.py:48
  302.7 0.7 constant_dynamic-update-slice_fusion.2
  303.5 0.9 constant_dynamic-slice_fusion.5
  304.4 0.9 copy.149
  306.7 14.9 %fusion.30 = f32[64,8,4,8]{1,3,2,0:T(8,128)S(1)} fusion(f32[1,64,8,4,8]{4,2,3,1,0:T(8,128)S(1)} %copy.149, f32[8]{0:T(128)S(1)} %compare_convert_fusion.2, f32[64,8,4]{1,2,0:T(4,128)S(1)} %bitcast.106, f32[4,64,8,8]{3,2,1,0:T(8,128)} %get-tuple-element.387, s32[]{:T(128)} %get-tuple-element.375), kind=kOutput, calls=%fused_computation.9.clone.1 | convolution fusion | flops 1605632 | bytes 401952 | tf_op jit(solution)/shard_map/while/body/eval_jaxpr/lij,locj->loci/dot_general | solution.py:48
  322.2 0.7 constant_dynamic-update-slice_fusion.2
  323.1 9.2 %while.29 = (s32[]{:T(128)}, f32[64,8,4]{0,2,1:T(4,128)S(1)}, f32[4,64,8,4,8]{1,4,3,2,0:T(8,128)S(1)}, f32[4,64,8,4,8]{1,4,3,2,0:T(8,128)}, f32[4]{0:T(128)S(1)}...) while((s32[]{:T(128)}, f32[64,8,4]{0,2,1:T(4,128)S(1)}, f32[4,64,8,4,8]{1,4,3,2,0:T(8,128)S(1)}, ...), condition=%wide.region_5.6_spmd, body=%wide.region_4.5_spmd.sunk | while | flops 38915 | bytes 459641 | solution.py:59
  324.4 0.9 subtract_dynamic-update-slice_fusion.2
  326.7 0.9 subtract_dynamic-update-slice_fusion.2
  329.0 0.9 subtract_dynamic-update-slice_fusion.2
  331.3 0.9 subtract_dynamic-update-slice_fusion.2
  332.3 0.9 copy.122
  (90 shorter events, 14.9 us)
Async XLA Ops:
  0.0 32.4 %copy-start = (bf16[1,2,96,3072]{3,2,1,0:T(8,128)(2,1)S(1)}, bf16[1,2,96,3072]{3,2,1,0:T(8,128)(2,1)}, u32[]{:S(2)}) copy-start(bf16[1,2,96,3072]{3,2,1,0:T(8,128)(2,1)} %param.10) | copy-start | bytes 3538948
  32.4 34.3 %copy-start.4 = (bf16[8,96,1024]{2,1,0:T(8,128)(2,1)S(1)}, bf16[8,96,1024]{2,1,0:T(8,128)(2,1)}, u32[]{:S(2)}) copy-start(bf16[8,96,1024]{2,1,0:T(8,128)(2,1)} %param.11) | copy-start | bytes 4718596
  37.2 25.8 %all-to-all-start.1 = ((bf16[1,96,256,2]{1,3,0,2:T(2,128)(2,1)}), bf16[1,96,256,2]{1,3,0,2:T(2,128)(2,1)S(1)}, u32[]{:S(2)}, u32[]{:S(2)}) async-start(bf16[1,96,256,2]{1,3,0,2:T(2,128)(2,1)} %copy.109), calls=%async_computation.1 | async-start | bytes 262144 | tf_op jit(solution)/shard_map/all_to_all | solution.py:82
  63.0 14.8 %all-to-all-start = ((bf16[1,96,256,2]{1,3,0,2:T(2,128)(2,1)}), bf16[1,96,256,2]{1,3,0,2:T(2,128)(2,1)S(1)}, u32[]{:S(2)}, u32[]{:S(2)}) async-start(bf16[1,96,256,2]{1,3,0,2:T(2,128)(2,1)} %copy.106), calls=%async_computation | async-start | bytes 262144 | tf_op jit(solution)/shard_map/all_to_all | solution.py:79
  77.8 55.7 %all-to-all-start.3 = ((bf16[8,96,1024]{1,0,2:T(8,128)(2,1)}), bf16[8,96,1024]{1,0,2:T(8,128)(2,1)S(1)}, u32[]{:S(2)}, u32[]{:S(2)}) async-start(bf16[8,96,1024]{1,0,2:T(8,128)(2,1)} %copy.112), calls=%async_computation.3 | async-start | bytes 4194304 | tf_op jit(solution)/shard_map/all_to_all | solution.py:86
  136.6 6.9 %copy-start.6 = (s32[256]{0:T(256)S(1)}, s32[256]{0:T(256)}, u32[]{:S(2)}) copy-start(s32[256]{0:T(256)} %param.12) | copy-start | bytes 3076
  136.6 8.9 %copy-start.5 = (f32[64,4,8,8]{0,3,2,1:T(8,128)S(1)}, f32[64,4,8,8]{0,3,2,1:T(8,128)}, u32[]{:S(2)}) copy-start(f32[64,4,8,8]{0,3,2,1:T(8,128)} %param.15) | copy-start | bytes 196612
  136.6 10.4 %copy-start.7 = (s32[256]{0:T(256)S(1)}, s32[256]{0:T(256)}, u32[]{:S(2)}) copy-start(s32[256]{0:T(256)} %param.13) | copy-start | bytes 3076
  136.6 101.4 %all-to-all-start.2 = ((bf16[16,32,2,96,8,2]{3,1,5,2,4,0:T(8,128)(2,1)}), bf16[16,32,2,96,8,2]{3,1,5,2,4,0:T(8,128)(2,1)}, u32[]{:S(2)}, u32[]{:S(2)}) async-start(bf16[16,32,2,96,8,2]{3,1,5,2,4,0:T(8,128)(2,1)} %stack.8), calls=%async_computation.2 | async-start | bytes 8388608 | tf_op jit(solution)/shard_map/all_to_all | solution.py:88
  241.5 1.0 copy-start.1
  241.5 1.2 copy-start.2
  241.5 1.3 copy-start.3
